TPU v7x, 32 devices: a whole 2x2x4 slice. The times are simulated.
32 devices in a mesh: grp: 2 (over x), row: 16 (over z, y, core).
Axes of the slice: x: 2, y: 2, z: 4, core: 2. Of those that a mesh axis runs over, the one named last changes fastest.
Arguments:
- blocks: float32 [1024, 7, 6, 6, 128], P(('grp', 'row')), parts along dimension 0, may hold values from -0.3 to 4.2
- couplings: int32 [1024, 4], P(('grp', 'row')), parts along dimension 0, may hold values from -1 to 511, as said below
- cotangent: float32 [1024, 6, 128], P(('grp', 'row')), parts along dimension 0, may hold values from -7.2 to 7.2
Outputs:
- adjoint: float32 [1024, 6, 128], P(('grp', 'row')), parts along dimension 0
- residual: float32 [1024, 6, 128], P(('grp', 'row')), parts along dimension 0
There are 2 independent parts, one for each index of `grp`. A program takes and returns all parts, laid end to end along the dimension named above; each array names one. Nothing has to cross between parts.
Inputs may be any that keep to these rules, and one draw needn't show every extreme that they name: With the device of tile t being t // 32: column 0 holds a tile of the next device, column 1 one of the previous device, column 2 one of the device 2 ahead, column 3 one of the device 2 behind; -1 exactly where that device lies outside the plate. Each column maps the tiles of one device one-to-one onto the tiles of its target device, and for s = couplings[t, k] >= 0, couplings[s, k'] = t, where k' pairs column 0 with 1 and 2 with 3.
All inputs are finite; a program needn't handle non-finite values.
Results may differ from a plain program's by a relative error of at most 0.0003.
Values sent between devices are 32-bit elements; how exact they have to be, the bound alone decides.
A program may use at most 64 MiB of HBM per device.

v0:
```python
import jax
import jax.numpy as jnp
from jax import lax
from jax.sharding import PartitionSpec as P

ITERS = 2


def padded(array, sides, width):
    for axis, dim in sides:
        count, length = (lax.axis_size(axis), array.shape[dim])
        up = [(i, (i + 1) % count) for i in range(count - 1)]
        down = [(j, i) for i, j in up]
        last = lax.slice_in_dim(array, length - width, length, axis=dim)
        leading = lax.slice_in_dim(array, 0, width, axis=dim)
        before = lax.ppermute(last, axis, up)
        after = lax.ppermute(leading, axis, down)
        array = jnp.concatenate([before, array, after], axis=dim)
    return array


def from_behind(array, axis, by):
    count = lax.axis_size(axis)
    pairs = [(i, i + by) for i in range(count) if 0 <= i + by < count]
    return lax.ppermute(array, axis, pairs)


def inner_sum(left, right):
    return jnp.sum(left * right)


def before_cell(values, incoming):
    last_cells = values[..., -1]
    moved = jnp.concatenate([incoming[None], last_cells[:-1]], axis=0)
    return jnp.concatenate([moved[..., None], values[..., :-1]], axis=-1)


def after_cell(values, incoming):
    first_cells = values[..., 0]
    moved = jnp.concatenate([first_cells[1:], incoming[None]], axis=0)
    return jnp.concatenate([values[..., 1:], moved[..., None]], axis=-1)


def pick_tiles(arrived, columns, tile_count):
    present = columns >= 0
    local_rows = jnp.where(present, columns % tile_count, 0)
    picked = arrived[local_rows]
    mask_shape = (columns.shape[0],) + (1,) * (arrived.ndim - 1)
    return jnp.where(present.reshape(mask_shape), picked, 0.0)


def local(blocks, couplings, cotangent):
    tile_count = blocks.shape[0]
    device_count = lax.axis_size("row")
    far_reach = max(2, device_count // 8)
    offsets = [1, -1, far_reach, -far_reach]
    paired = [1, 0, 3, 2]
    edges = jnp.stack([blocks[0, 1, :, :, 0], blocks[-1, 2, :, :, -1]], axis=0)
    rimmed = padded(edges, (("row", 0),), 1)
    slots = [
        blocks[:, 0],
        before_cell(blocks[:, 2], rimmed[0]),
        after_cell(blocks[:, 1], rimmed[3]),
    ]
    for column in range(4):
        arrived = from_behind(blocks[:, 3 + paired[column]], "row", -offsets[column])
        slots.append(pick_tiles(arrived, couplings[:, column], tile_count))
    transposed = jnp.swapaxes(jnp.stack(slots, axis=1), 2, 3)

    def apply_adjoint(field):
        field_edges = jnp.stack([field[0, :, 0], field[-1, :, -1]], axis=0)
        rimmed_field = padded(field_edges, (("row", 0),), 1)
        nearby = [field, before_cell(field, rimmed_field[0]), after_cell(field, rimmed_field[3])]
        for column in range(4):
            arrived_field = from_behind(field, "row", -offsets[column])
            nearby.append(pick_tiles(arrived_field, couplings[:, column], tile_count))
        stacked = jnp.stack(nearby, axis=1)
        return jnp.sum(transposed * stacked[:, :, None], axis=(1, 3))

    adjoint = jnp.zeros_like(cotangent)
    residual = cotangent
    direction = cotangent
    rho_now = lax.psum(inner_sum(cotangent, residual), "row")
    for iteration in range(ITERS):
        image_dir = apply_adjoint(direction)
        alpha_step = rho_now / lax.psum(inner_sum(cotangent, image_dir), "row")
        half_step = residual - alpha_step * image_dir
        bent_image = apply_adjoint(half_step)
        tilt_sum, square_sum = lax.psum(
            (inner_sum(bent_image, half_step), inner_sum(bent_image, bent_image)), "row"
        )
        omega_step = tilt_sum / square_sum
        adjoint = adjoint + alpha_step * direction + omega_step * half_step
        residual = half_step - omega_step * bent_image
        if iteration + 1 < ITERS:
            rho_next = lax.psum(inner_sum(cotangent, residual), "row")
        if iteration + 1 < ITERS:
            direction = residual + rho_next / rho_now * (alpha_step / omega_step) * (
                direction - omega_step * image_dir
            )
            rho_now = rho_next
    return (adjoint, residual)


def solution(mesh):
    placed = (
        P(("grp", "row"), None, None, None, None),
        P(("grp", "row"), None),
        P(("grp", "row"), None, None),
    )
    return jax.shard_map(
        local,
        mesh=mesh,
        in_specs=placed,
        out_specs=(P(("grp", "row"), None, None), P(("grp", "row"), None, None)),
        check_vma=False,
    )
```

profile of v0, /device:TPU:0, one launch (start us, length us, event | category | flops | bytes accessed | tf_op | source)
XLA Modules:
  0.0 350.8 jit_solution(4609193442930322394)
XLA Ops:
  2.9 3.7 %collective-permute-start.9 = (f32[32,6,128]{2,1,0:T(8,128)S(1)}, f32[32,6,128]{2,1,0:T(8,128)}, u32[]{:S(2)}, u32[]{:S(2)}) collective-permute-start(f32[32,6,128]{2,1,0:T(8,128)S(1)} %copy.211), channel_id=1, source_target_pairs={{0,1},{1,2},{2,3},{3,4},{4,5},{5,6},{6,7},{7,8},{8,9},{9,10},{10,1... | collective-permute-start | bytes 294920 | tf_op jit(solution)/shard_map/ppermute | solution.py:25
  7.9 5.5 %collective-permute-start.11 = (f32[32,6,128]{2,1,0:T(8,128)S(1)}, f32[32,6,128]{2,1,0:T(8,128)}, u32[]{:S(2)}, u32[]{:S(2)}) collective-permute-start(f32[32,6,128]{2,1,0:T(8,128)S(1)} %copy.211), channel_id=1, source_target_pairs={{0,2},{1,3},{2,4},{3,5},{4,6},{5,7},{6,8},{7,9},{8,10},{9,11},{10,... | collective-permute-start | bytes 294920 | tf_op jit(solution)/shard_map/ppermute | solution.py:25
  14.4 3.7 %collective-permute-start.6 = (f32[1,6]{1,0:T(1,128)S(1)}, f32[1,6]{1,0:T(1,128)S(1)}, u32[]{:S(2)}, u32[]{:S(2)}) collective-permute-start(f32[1,6]{1,0:T(1,128)S(1)} %bitcast.219), channel_id=1, source_target_pairs={{0,1},{1,2},{2,3},{3,4},{4,5},{5,6},{6,7},{7,8},{8,9},{9,10},{10,1... | collective-permute-start | bytes 80 | tf_op jit(solution)/shard_map/ppermute | solution.py:16
  18.1 3.9 %slice_bitcast_fusion = (f32[32,6,6,128]{3,0,2,1:T(8,128)}, f32[32,1,6,6,128]{4,0,3,2,1:T(8,128)S(1)}, f32[32,1,6,6,128]{4,0,3,2,1:T(8,128)}, f32[32,6,6,128]{3,...) fusion(f32[32,7,6,6,128]{4,0,3,2,1:T(8,128)} %param.3), kind=kLoop, calls=%fused_computation.39 | loop fusion | bytes 8257536 | tf_op jit(solution)/shard_map/squeeze | solution.py:66
  35.9 4.2 %collective-permute-start = (f32[1,6,6]{2,0,1:T(1,128)S(1)}, f32[1,6,6]{2,0,1:T(1,128)S(1)}, u32[]{:S(2)}, u32[]{:S(2)}) collective-permute-start(f32[1,6,6]{2,0,1:T(1,128)S(1)} %stack_squeeze.30), channel_id=1, source_target_pairs={{0,1},{1,2},{2,3},{3,4},{4,5},{5,6},{6,7},{7,8},{8,9},{9,10},{10,1... | collective-permute-start | bytes 440 | tf_op jit(solution)/shard_map/ppermute | solution.py:16
  50.1 5.2 %collective-permute-start.3 = (f32[32,6,6,128]{3,0,2,1:T(8,128)}, f32[32,6,6,128]{3,0,2,1:T(8,128)S(1)}, u32[]{:S(2)}, u32[]{:S(2)}) collective-permute-start(f32[32,6,6,128]{3,0,2,1:T(8,128)} %get-tuple-element.32), channel_id=1, source_target_pairs={{0,1},{1,2},{2,3},{3,4},{4,5},{5,6},{6,7},{7,8},{8,9},{9,10},{10,1... | collective-permute-start | bytes 1769480 | tf_op jit(solution)/shard_map/ppermute | solution.py:25
  60.3 5.9 %collective-permute-start.5 = (f32[32,6,6,128]{3,0,2,1:T(8,128)}, f32[32,6,6,128]{3,0,2,1:T(8,128)}, u32[]{:S(2)}, u32[]{:S(2)}) collective-permute-start(f32[32,6,6,128]{3,0,2,1:T(8,128)} %get-tuple-element.28), channel_id=1, source_target_pairs={{0,2},{1,3},{2,4},{3,5},{4,6},{5,7},{6,8},{7,9},{8,10},{9,11},{10,... | collective-permute-start | bytes 1769480 | tf_op jit(solution)/shard_map/ppermute | solution.py:25
  76.5 13.2 %collective-permute-done.5 = f32[32,6,6,128]{3,0,2,1:T(8,128)} collective-permute-done((f32[32,6,6,128]{3,0,2,1:T(8,128)}, f32[32,6,6,128]{3,0,2,1:T(8,128)}, u32[]{:S(2)}, u32[]{:S(2)}) %collective-permute-start.5) | collective-permute-done | bytes 589856 | tf_op jit(solution)/shard_map/ppermute | solution.py:25
  97.9 3.7 %multiply_reduce_fusion.3 = f32[32,6,128]{2,1,0:T(8,128)S(1)} fusion(f32[32,7,6,6,128]{4,3,2,0,1:T(8,128)} %fusion.2, f32[32,7,6,128]{3,2,0,1:T(8,128)S(1)} %copy-done.1), kind=kLoop, calls=%fused_computation.23 | loop fusion | flops 2039808 | bytes 4915200 | tf_op jit(solution)/shard_map/reduce_sum | solution.py:78
  102.2 38.0 %all-reduce.2 = (f32[]{:T(128)}, f32[]{:T(128)}) all-reduce(f32[]{:T(128)} %multiply_reduce_fusion.11, f32[]{:T(128)} %multiply_reduce_fusion.10), channel_id=1, replica_groups=mesh['grp'=2,'row'=16] {'row'}, use_global_device_ids=true, to_apply=%region_1.2 | all-reduce | flops 2 | bytes 16 | tf_op jit(solution)/shard_map/psum | solution.py:83
  147.7 4.6 %collective-permute-start.17 = (f32[32,6,128]{2,1,0:T(8,128)S(1)}, f32[32,6,128]{2,1,0:T(8,128)S(1)}, u32[]{:S(2)}, u32[]{:S(2)}) collective-permute-start(f32[32,6,128]{2,1,0:T(8,128)S(1)} %get-tuple-element.27), channel_id=1, source_target_pairs={{0,2},{1,3},{2,4},{3,5},{4,6},{5,7},{6,8},{7,9},{8,10},{9,11},{10,... | collective-permute-start | bytes 294920 | tf_op jit(solution)/shard_map/ppermute | solution.py:25
  155.4 3.2 collective-permute-start.12
  162.8 3.4 multiply_reduce_fusion.2
  166.9 30.5 %all-reduce.1 = (f32[]{:T(128)}, f32[]{:T(128)}) all-reduce(f32[]{:T(128)} %get-tuple-element.13, f32[]{:T(128)} %get-tuple-element.12), channel_id=1, replica_groups=mesh['grp'=2,'row'=16] {'row'}, use_global_device_ids=true, to_apply=%region_7.8 | all-reduce | flops 2 | bytes 16 | tf_op jit(solution)/shard_map/psum | solution.py:89
  201.9 30.1 %psum.60 = f32[]{:T(128)} all-reduce(f32[]{:T(128)} %multiply_reduce_fusion.7), channel_id=1, replica_groups=mesh['grp'=2,'row'=16] {'row'}, use_global_device_ids=true, to_apply=%region_11.12 | all-reduce | flops 1 | bytes 8 | tf_op jit(solution)/shard_map/psum | solution.py:96
  235.2 3.0 collective-permute-start.21
  239.5 4.6 %collective-permute-start.23 = (f32[32,6,128]{2,1,0:T(8,128)S(1)}, f32[32,6,128]{2,1,0:T(8,128)S(1)}, u32[]{:S(2)}, u32[]{:S(2)}) collective-permute-start(f32[32,6,128]{2,1,0:T(8,128)S(1)} %get-tuple-element.25), channel_id=1, source_target_pairs={{0,2},{1,3},{2,4},{3,5},{4,6},{5,7},{6,8},{7,9},{8,10},{9,11},{10,... | collective-permute-start | bytes 294920 | tf_op jit(solution)/shard_map/ppermute | solution.py:25
  247.3 4.3 %collective-permute-start.18 = (f32[1,6]{1,0:T(1,128)S(1)}, f32[1,6]{1,0:T(1,128)S(1)}, u32[]{:S(2)}, u32[]{:S(2)}) collective-permute-start(f32[1,6]{1,0:T(1,128)S(1)} %bitcast.221), channel_id=1, source_target_pairs={{0,1},{1,2},{2,3},{3,4},{4,5},{5,6},{6,7},{7,8},{8,9},{9,10},{10,1... | collective-permute-start | bytes 80 | tf_op jit(solution)/shard_map/ppermute | solution.py:16
  255.8 3.4 multiply_reduce_fusion.1
  259.8 30.4 %psum.61 = f32[]{:T(128)} all-reduce(f32[]{:T(128)} %multiply_reduce_fusion.6), channel_id=1, replica_groups=mesh['grp'=2,'row'=16] {'row'}, use_global_device_ids=true, to_apply=%region_14.15 | all-reduce | flops 1 | bytes 8 | tf_op jit(solution)/shard_map/psum | solution.py:86
  297.6 4.6 %collective-permute-start.29 = (f32[32,6,128]{2,1,0:T(8,128)S(1)}, f32[32,6,128]{2,1,0:T(8,128)S(1)}, u32[]{:S(2)}, u32[]{:S(2)}) collective-permute-start(f32[32,6,128]{2,1,0:T(8,128)S(1)} %get-tuple-element.23), channel_id=1, source_target_pairs={{0,2},{1,3},{2,4},{3,5},{4,6},{5,7},{6,8},{7,9},{8,10},{9,11},{10,... | collective-permute-start | bytes 294920 | tf_op jit(solution)/shard_map/ppermute | solution.py:25
  305.4 4.0 %collective-permute-start.24 = (f32[1,6]{1,0:T(1,128)S(1)}, f32[1,6]{1,0:T(1,128)S(1)}, u32[]{:S(2)}, u32[]{:S(2)}) collective-permute-start(f32[1,6]{1,0:T(1,128)S(1)} %bitcast.222), channel_id=1, source_target_pairs={{0,1},{1,2},{2,3},{3,4},{4,5},{5,6},{6,7},{7,8},{8,9},{9,10},{10,1... | collective-permute-start | bytes 80 | tf_op jit(solution)/shard_map/ppermute | solution.py:16
  313.6 3.4 multiply_reduce_fusion
  317.6 30.4 %all-reduce = (f32[]{:T(128)}, f32[]{:T(128)}) all-reduce(f32[]{:T(128)} %get-tuple-element.11, f32[]{:T(128)} %get-tuple-element.10), channel_id=1, replica_groups=mesh['grp'=2,'row'=16] {'row'}, use_global_device_ids=true, to_apply=%region_17.18 | all-reduce | flops 2 | bytes 16 | tf_op jit(solution)/shard_map/psum | solution.py:89
  (183 shorter events, 93.1 us)
Async XLA Ops:
  1.6 48.5 %collective-permute-start.8 = (f32[32,6,128]{2,1,0:T(8,128)S(1)}, f32[32,6,128]{2,1,0:T(8,128)}, u32[]{:S(2)}, u32[]{:S(2)}) collective-permute-start(f32[32,6,128]{2,1,0:T(8,128)S(1)} %copy.211), channel_id=1, source_target_pairs={{1,0},{2,1},{3,2},{4,3},{5,4},{6,5},{7,6},{8,7},{9,8},{10,9},{11,1... | collective-permute-start | bytes 294920 | tf_op jit(solution)/shard_map/ppermute | solution.py:25
  2.9 54.6 %collective-permute-start.9 = (f32[32,6,128]{2,1,0:T(8,128)S(1)}, f32[32,6,128]{2,1,0:T(8,128)}, u32[]{:S(2)}, u32[]{:S(2)}) collective-permute-start(f32[32,6,128]{2,1,0:T(8,128)S(1)} %copy.211), channel_id=1, source_target_pairs={{0,1},{1,2},{2,3},{3,4},{4,5},{5,6},{6,7},{7,8},{8,9},{9,10},{10,1... | collective-permute-start | bytes 294920 | tf_op jit(solution)/shard_map/ppermute | solution.py:25
  6.6 53.7 %collective-permute-start.10 = (f32[32,6,128]{2,1,0:T(8,128)S(1)}, f32[32,6,128]{2,1,0:T(8,128)}, u32[]{:S(2)}, u32[]{:S(2)}) collective-permute-start(f32[32,6,128]{2,1,0:T(8,128)S(1)} %copy.211), channel_id=1, source_target_pairs={{2,0},{3,1},{4,2},{5,3},{6,4},{7,5},{8,6},{9,7},{10,8},{11,9},{12,... | collective-permute-start | bytes 294920 | tf_op jit(solution)/shard_map/ppermute | solution.py:25
  7.9 59.8 %collective-permute-start.11 = (f32[32,6,128]{2,1,0:T(8,128)S(1)}, f32[32,6,128]{2,1,0:T(8,128)}, u32[]{:S(2)}, u32[]{:S(2)}) collective-permute-start(f32[32,6,128]{2,1,0:T(8,128)S(1)} %copy.211), channel_id=1, source_target_pairs={{0,2},{1,3},{2,4},{3,5},{4,6},{5,7},{6,8},{7,9},{8,10},{9,11},{10,... | collective-permute-start | bytes 294920 | tf_op jit(solution)/shard_map/ppermute | solution.py:25
  14.4 18.3 %collective-permute-start.6 = (f32[1,6]{1,0:T(1,128)S(1)}, f32[1,6]{1,0:T(1,128)S(1)}, u32[]{:S(2)}, u32[]{:S(2)}) collective-permute-start(f32[1,6]{1,0:T(1,128)S(1)} %bitcast.219), channel_id=1, source_target_pairs={{0,1},{1,2},{2,3},{3,4},{4,5},{5,6},{6,7},{7,8},{8,9},{9,10},{10,1... | collective-permute-start | bytes 80 | tf_op jit(solution)/shard_map/ppermute | solution.py:16
  35.9 7.0 %collective-permute-start = (f32[1,6,6]{2,0,1:T(1,128)S(1)}, f32[1,6,6]{2,0,1:T(1,128)S(1)}, u32[]{:S(2)}, u32[]{:S(2)}) collective-permute-start(f32[1,6,6]{2,0,1:T(1,128)S(1)} %stack_squeeze.30), channel_id=1, source_target_pairs={{0,1},{1,2},{2,3},{3,4},{4,5},{5,6},{6,7},{7,8},{8,9},{9,10},{10,1... | collective-permute-start | bytes 440 | tf_op jit(solution)/shard_map/ppermute | solution.py:16
  45.9 25.5 %collective-permute-start.2 = (f32[32,6,6,128]{3,0,2,1:T(8,128)}, f32[32,6,6,128]{3,0,2,1:T(8,128)}, u32[]{:S(2)}, u32[]{:S(2)}) collective-permute-start(f32[32,6,6,128]{3,0,2,1:T(8,128)} %get-tuple-element.31), channel_id=1, source_target_pairs={{1,0},{2,1},{3,2},{4,3},{5,4},{6,5},{7,6},{8,7},{9,8},{10,9},{11,1... | collective-permute-start | bytes 1769480 | tf_op jit(solution)/shard_map/ppermute | solution.py:25
  50.1 23.4 %collective-permute-start.3 = (f32[32,6,6,128]{3,0,2,1:T(8,128)}, f32[32,6,6,128]{3,0,2,1:T(8,128)S(1)}, u32[]{:S(2)}, u32[]{:S(2)}) collective-permute-start(f32[32,6,6,128]{3,0,2,1:T(8,128)} %get-tuple-element.32), channel_id=1, source_target_pairs={{0,1},{1,2},{2,3},{3,4},{4,5},{5,6},{6,7},{7,8},{8,9},{9,10},{10,1... | collective-permute-start | bytes 1769480 | tf_op jit(solution)/shard_map/ppermute | solution.py:25
  57.5 16.9 %collective-permute-start.4 = (f32[32,6,6,128]{3,0,2,1:T(8,128)}, f32[32,6,6,128]{3,0,2,1:T(8,128)}, u32[]{:S(2)}, u32[]{:S(2)}) collective-permute-start(f32[32,6,6,128]{3,0,2,1:T(8,128)} %get-tuple-element.34), channel_id=1, source_target_pairs={{2,0},{3,1},{4,2},{5,3},{6,4},{7,5},{8,6},{9,7},{10,8},{11,9},{12,... | collective-permute-start | bytes 1769480 | tf_op jit(solution)/shard_map/ppermute | solution.py:25
  60.3 29.4 %collective-permute-start.5 = (f32[32,6,6,128]{3,0,2,1:T(8,128)}, f32[32,6,6,128]{3,0,2,1:T(8,128)}, u32[]{:S(2)}, u32[]{:S(2)}) collective-permute-start(f32[32,6,6,128]{3,0,2,1:T(8,128)} %get-tuple-element.28), channel_id=1, source_target_pairs={{0,2},{1,3},{2,4},{3,5},{4,6},{5,7},{6,8},{7,9},{8,10},{9,11},{10,... | collective-permute-start | bytes 1769480 | tf_op jit(solution)/shard_map/ppermute | solution.py:25
  142.0 17.9 %collective-permute-start.14 = (f32[32,6,128]{2,1,0:T(8,128)S(1)}, f32[32,6,128]{2,1,0:T(8,128)S(1)}, u32[]{:S(2)}, u32[]{:S(2)}) collective-permute-start(f32[32,6,128]{2,1,0:T(8,128)S(1)} %get-tuple-element.27), channel_id=1, source_target_pairs={{1,0},{2,1},{3,2},{4,3},{5,4},{6,5},{7,6},{8,7},{9,8},{10,9},{11,1... | collective-permute-start | bytes 294920 | tf_op jit(solution)/shard_map/ppermute | solution.py:25
  143.3 17.4 %collective-permute-start.15 = (f32[32,6,128]{2,1,0:T(8,128)S(1)}, f32[32,6,128]{2,1,0:T(8,128)S(1)}, u32[]{:S(2)}, u32[]{:S(2)}) collective-permute-start(f32[32,6,128]{2,1,0:T(8,128)S(1)} %get-tuple-element.27), channel_id=1, source_target_pairs={{0,1},{1,2},{2,3},{3,4},{4,5},{5,6},{6,7},{7,8},{8,9},{9,10},{10,1... | collective-permute-start | bytes 294920 | tf_op jit(solution)/shard_map/ppermute | solution.py:25
  146.4 15.0 %collective-permute-start.16 = (f32[32,6,128]{2,1,0:T(8,128)S(1)}, f32[32,6,128]{2,1,0:T(8,128)S(1)}, u32[]{:S(2)}, u32[]{:S(2)}) collective-permute-start(f32[32,6,128]{2,1,0:T(8,128)S(1)} %get-tuple-element.27), channel_id=1, source_target_pairs={{2,0},{3,1},{4,2},{5,3},{6,4},{7,5},{8,6},{9,7},{10,8},{11,9},{12,... | collective-permute-start | bytes 294920 | tf_op jit(solution)/shard_map/ppermute | solution.py:25
  147.7 14.4 %collective-permute-start.17 = (f32[32,6,128]{2,1,0:T(8,128)S(1)}, f32[32,6,128]{2,1,0:T(8,128)S(1)}, u32[]{:S(2)}, u32[]{:S(2)}) collective-permute-start(f32[32,6,128]{2,1,0:T(8,128)S(1)} %get-tuple-element.27), channel_id=1, source_target_pairs={{0,2},{1,3},{2,4},{3,5},{4,6},{5,7},{6,8},{7,9},{8,10},{9,11},{10,... | collective-permute-start | bytes 294920 | tf_op jit(solution)/shard_map/ppermute | solution.py:25
  233.9 19.0 %collective-permute-start.20 = (f32[32,6,128]{2,1,0:T(8,128)S(1)}, f32[32,6,128]{2,1,0:T(8,128)S(1)}, u32[]{:S(2)}, u32[]{:S(2)}) collective-permute-start(f32[32,6,128]{2,1,0:T(8,128)S(1)} %get-tuple-element.25), channel_id=1, source_target_pairs={{1,0},{2,1},{3,2},{4,3},{5,4},{6,5},{7,6},{8,7},{9,8},{10,9},{11,1... | collective-permute-start | bytes 294920 | tf_op jit(solution)/shard_map/ppermute | solution.py:25
  235.2 18.4 %collective-permute-start.21 = (f32[32,6,128]{2,1,0:T(8,128)S(1)}, f32[32,6,128]{2,1,0:T(8,128)S(1)}, u32[]{:S(2)}, u32[]{:S(2)}) collective-permute-start(f32[32,6,128]{2,1,0:T(8,128)S(1)} %get-tuple-element.25), channel_id=1, source_target_pairs={{0,1},{1,2},{2,3},{3,4},{4,5},{5,6},{6,7},{7,8},{8,9},{9,10},{10,1... | collective-permute-start | bytes 294920 | tf_op jit(solution)/shard_map/ppermute | solution.py:25
  238.2 16.1 %collective-permute-start.22 = (f32[32,6,128]{2,1,0:T(8,128)S(1)}, f32[32,6,128]{2,1,0:T(8,128)S(1)}, u32[]{:S(2)}, u32[]{:S(2)}) collective-permute-start(f32[32,6,128]{2,1,0:T(8,128)S(1)} %get-tuple-element.25), channel_id=1, source_target_pairs={{2,0},{3,1},{4,2},{5,3},{6,4},{7,5},{8,6},{9,7},{10,8},{11,9},{12,... | collective-permute-start | bytes 294920 | tf_op jit(solution)/shard_map/ppermute | solution.py:25
  239.5 15.5 %collective-permute-start.23 = (f32[32,6,128]{2,1,0:T(8,128)S(1)}, f32[32,6,128]{2,1,0:T(8,128)S(1)}, u32[]{:S(2)}, u32[]{:S(2)}) collective-permute-start(f32[32,6,128]{2,1,0:T(8,128)S(1)} %get-tuple-element.25), channel_id=1, source_target_pairs={{0,2},{1,3},{2,4},{3,5},{4,6},{5,7},{6,8},{7,9},{8,10},{9,11},{10,... | collective-permute-start | bytes 294920 | tf_op jit(solution)/shard_map/ppermute | solution.py:25
  247.3 5.1 %collective-permute-start.18 = (f32[1,6]{1,0:T(1,128)S(1)}, f32[1,6]{1,0:T(1,128)S(1)}, u32[]{:S(2)}, u32[]{:S(2)}) collective-permute-start(f32[1,6]{1,0:T(1,128)S(1)} %bitcast.221), channel_id=1, source_target_pairs={{0,1},{1,2},{2,3},{3,4},{4,5},{5,6},{6,7},{7,8},{8,9},{9,10},{10,1... | collective-permute-start | bytes 80 | tf_op jit(solution)/shard_map/ppermute | solution.py:16
  292.0 18.7 %collective-permute-start.26 = (f32[32,6,128]{2,1,0:T(8,128)S(1)}, f32[32,6,128]{2,1,0:T(8,128)S(1)}, u32[]{:S(2)}, u32[]{:S(2)}) collective-permute-start(f32[32,6,128]{2,1,0:T(8,128)S(1)} %get-tuple-element.23), channel_id=1, source_target_pairs={{1,0},{2,1},{3,2},{4,3},{5,4},{6,5},{7,6},{8,7},{9,8},{10,9},{11,1... | collective-permute-start | bytes 294920 | tf_op jit(solution)/shard_map/ppermute | solution.py:25
  293.3 18.1 %collective-permute-start.27 = (f32[32,6,128]{2,1,0:T(8,128)S(1)}, f32[32,6,128]{2,1,0:T(8,128)S(1)}, u32[]{:S(2)}, u32[]{:S(2)}) collective-permute-start(f32[32,6,128]{2,1,0:T(8,128)S(1)} %get-tuple-element.23), channel_id=1, source_target_pairs={{0,1},{1,2},{2,3},{3,4},{4,5},{5,6},{6,7},{7,8},{8,9},{9,10},{10,1... | collective-permute-start | bytes 294920 | tf_op jit(solution)/shard_map/ppermute | solution.py:25
  296.3 15.8 %collective-permute-start.28 = (f32[32,6,128]{2,1,0:T(8,128)S(1)}, f32[32,6,128]{2,1,0:T(8,128)S(1)}, u32[]{:S(2)}, u32[]{:S(2)}) collective-permute-start(f32[32,6,128]{2,1,0:T(8,128)S(1)} %get-tuple-element.23), channel_id=1, source_target_pairs={{2,0},{3,1},{4,2},{5,3},{6,4},{7,5},{8,6},{9,7},{10,8},{11,9},{12,... | collective-permute-start | bytes 294920 | tf_op jit(solution)/shard_map/ppermute | solution.py:25
  297.6 15.2 %collective-permute-start.29 = (f32[32,6,128]{2,1,0:T(8,128)S(1)}, f32[32,6,128]{2,1,0:T(8,128)S(1)}, u32[]{:S(2)}, u32[]{:S(2)}) collective-permute-start(f32[32,6,128]{2,1,0:T(8,128)S(1)} %get-tuple-element.23), channel_id=1, source_target_pairs={{0,2},{1,3},{2,4},{3,5},{4,6},{5,7},{6,8},{7,9},{8,10},{9,11},{10,... | collective-permute-start | bytes 294920 | tf_op jit(solution)/shard_map/ppermute | solution.py:25
  305.4 4.8 %collective-permute-start.24 = (f32[1,6]{1,0:T(1,128)S(1)}, f32[1,6]{1,0:T(1,128)S(1)}, u32[]{:S(2)}, u32[]{:S(2)}) collective-permute-start(f32[1,6]{1,0:T(1,128)S(1)} %bitcast.222), channel_id=1, source_target_pairs={{0,1},{1,2},{2,3},{3,4},{4,5},{5,6},{6,7},{7,8},{8,9},{9,10},{10,1... | collective-permute-start | bytes 80 | tf_op jit(solution)/shard_map/ppermute | solution.py:16
  (9 other events, 43.5 us)
where the time goes:
time: 353 us; the launch traced here: 351 us
  blocking collectives  159 us (45%)
  starting transfers between devices  81.8 us (23%)
  local copies, waits for them, and re-layouts  43.5 us (12%)
  other arithmetic  32.6 us (9%)
  waiting for transfers between devices  22.6 us (6%)
  between operations  10.8 us (3%)
    psum x2, blocking collectives, local(): lax.psum((inner_sum(bent_image, half_step), inner_sum(bent_image, bent_im...  60.9 us
    ppermute x20, starting transfers between devices, from_behind(): return lax.ppermute(array, axis, pairs)  56 us
    psum x1, blocking collectives, local(): rho_now = lax.psum(inner_sum(cotangent, residual), 'row')  38 us
    psum x1, blocking collectives, local(): alpha_step = rho_now / lax.psum(inner_sum(cotangent, image_dir), 'row')  30.4 us
    psum x1, blocking collectives, local(): rho_next = lax.psum(inner_sum(cotangent, residual), 'row')  30.1 us
    ppermute x5, starting transfers between devices, padded(): before = lax.ppermute(last, axis, up)  19.4 us
    gather x20, local copies, waits for them, and re-layouts, pick_tiles(): picked = arrived[local_rows]  16.4 us
    reduce_sum x4, other arithmetic, apply_adjoint(): return jnp.sum(transposed * stacked[:, :, None], axis=(1, 3))  13.8 us
  transfers between devices with their start and end apart: 30, of which 9 were waited for; matrix products, arithmetic and copies ran while one was open for 13% of the time, Pallas kernels for 0%

commit v1 on v0

v1 whole, which is shorter than its diff:
```python
import functools

import jax
import jax.numpy as jnp
from jax import lax
from jax.experimental import pallas as pl
from jax.experimental.pallas import tpu as pltpu
from jax.sharding import PartitionSpec as P

MESH = pl.DeviceIdType.MESH
PAIRED = (1, 0, 3, 2)
ORDER = (2, 3, 0, 1)
GROUP = 8


def kernel(
    n, far, blocks_hbm, coup, b_ref, adj_ref, res_ref,
    blk, edge_blk, img, img2, bent, bent_img, direc, half,
    left, right, send, red_send, red,
    load_sem, send_sem, recv_sem, red_send_sem, red_recv_sem, *arrivals,
):
    recv = [arrivals[4 * step:4 * step + 4] for step in range(4)]
    tiles, fields, cells = b_ref.shape
    me = lax.axis_index("row")
    offsets = (1, -1, far, -far)
    last = tiles - 1

    def load(slot):
        return pltpu.make_async_copy(blocks_hbm.at[:, slot], blk.at[slot], load_sem.at[slot])

    edge_loads = (
        pltpu.make_async_copy(blocks_hbm.at[last, 2], edge_blk.at[0], load_sem.at[7]),
        pltpu.make_async_copy(blocks_hbm.at[0, 1], edge_blk.at[1], load_sem.at[8]),
    )
    load(5).start()
    load(6).start()
    edge_loads[0].start()
    edge_loads[1].start()
    for slot in (3, 4, 1, 2, 0):
        load(slot).start()

    barrier = pltpu.get_barrier_semaphore()

    def greet(i, carry):
        other = lax.rem(me + i, n)
        pl.semaphore_signal(barrier, inc=1, device_id={"row": other}, device_id_type=MESH)
        return carry

    lax.fori_loop(1, n, greet, 0)

    def has_target(j):
        to = me + offsets[j]
        return jnp.logical_and(to >= 0, to < n)

    def has_source(j):
        origin = me - offsets[j]
        return jnp.logical_and(origin >= 0, origin < n)

    for j in range(4):
        @pl.when(jnp.logical_not(has_source(j)))
        def _():
            for step in range(4):
                recv[step][j][...] = jnp.zeros(recv[step][j].shape, jnp.float32)

    def message(step, j):
        return pltpu.make_async_remote_copy(
            src_ref=send.at[step, j],
            dst_ref=recv[step][j],
            send_sem=send_sem.at[step, j],
            recv_sem=recv_sem.at[step, j],
            device_id={"row": me + offsets[j]},
            device_id_type=MESH,
        )

    lane = lax.broadcasted_iota(jnp.int32, (fields, cells), 1)
    first_lane = lane == 0
    last_lane = lane == cells - 1

    def product(field, slot, rows):
        total = None
        for a in range(fields):
            term = blk[slot, rows, a] * field[rows, pl.ds(a, 1), :]
            total = term if total is None else total + term
        return total

    def edge_product(field, which, tile):
        total = None
        for a in range(fields):
            term = edge_blk[which, a] * field[tile, pl.ds(a, 1), :]
            total = term if total is None else total + term
        return total

    def send_channels(step, field):
        for j in ORDER:
            if step == 0:
                load(3 + j).wait()

            @pl.loop(0, tiles // GROUP)
            def _(chunk):
                rows = pl.ds(chunk * GROUP, GROUP)
                send[step, j, rows] = product(field, 3 + j, rows)

            if j < 2:
                if step == 0:
                    edge_loads[j].wait()
                edge = edge_product(field, j, last if j == 0 else 0)
                send[step, j, tiles] = pltpu.roll(edge, 1 if j == 0 else cells - 1, 1)
            else:
                send[step, j, tiles] = jnp.zeros((fields, cells), jnp.float32)
            if step == 0 and j == ORDER[0]:
                pl.semaphore_wait(barrier, n - 1)

            @pl.when(has_target(j))
            def _():
                message(step, j).start()

    def local_part(step, field, out):
        if step == 0:
            for slot in (1, 2, 0):
                load(slot).wait()
            left[tiles] = jnp.zeros((fields, cells), jnp.float32)
            right[0] = jnp.zeros((fields, cells), jnp.float32)

        @pl.loop(0, tiles // GROUP)
        def _(chunk):
            rows = pl.ds(chunk * GROUP, GROUP)
            left[rows] = pltpu.roll(product(field, 1, rows), cells - 1, 2)
            right[pl.ds(chunk * GROUP + 1, GROUP)] = pltpu.roll(product(field, 2, rows), 1, 2)
            out[rows] = product(field, 0, rows)

        @pl.loop(0, tiles // GROUP)
        def _(chunk):
            rows = pl.ds(chunk * GROUP, GROUP)
            after = pl.ds(chunk * GROUP + 1, GROUP)
            out[rows] = (
                out[rows]
                + jnp.where(last_lane, left[after], left[rows])
                + jnp.where(first_lane, right[rows], right[after])
            )

    def receive(step, out):
        for j in ORDER:
            @pl.when(has_source(j))
            def _():
                message(step, j).wait_recv()

            @pl.loop(0, tiles // GROUP)
            def _(chunk):
                for i in range(GROUP):
                    tile = chunk * GROUP + i
                    origin = jnp.bitwise_and(coup[tile, PAIRED[j]], tiles - 1)
                    out[tile] = out[tile] + recv[step][j][origin]

        out[0] = out[0] + jnp.where(first_lane, recv[step][0][tiles], 0.0)
        out[last] = out[last] + jnp.where(last_lane, recv[step][1][tiles], 0.0)

    def partial_copy(step, other, origin):
        return pltpu.make_async_remote_copy(
            src_ref=red_send.at[step],
            dst_ref=red.at[step, origin],
            send_sem=red_send_sem.at[step, other],
            recv_sem=red_recv_sem.at[step, origin],
            device_id={"row": other},
            device_id_type=MESH,
        )

    def share(step, pairs):
        rows = [
            jnp.sum(jnp.sum(x * y, axis=0), axis=0, keepdims=True) for x, y in pairs
        ]
        rows += [jnp.zeros((8 - len(rows), cells), jnp.float32)]
        tile = jnp.concatenate(rows, axis=0)
        red_send[step] = tile
        red[step, me] = tile

        def go(i, carry):
            partial_copy(step, lax.rem(me + i, n), me).start()
            return carry

        lax.fori_loop(1, n, go, 0)

    def collect(step, count):
        def arrive(i, carry):
            other = lax.rem(me + i, n)
            partial_copy(step, other, other).wait_recv()
            return carry

        lax.fori_loop(1, n, arrive, 0)
        total = jnp.sum(jnp.sum(red[step], axis=0), axis=1, keepdims=True)
        return [total[q:q + 1] for q in range(count)]

    send_channels(0, b_ref)
    local_part(0, b_ref, img)
    receive(0, img)
    b = b_ref[...]
    share(0, [(b, b), (b, img[...])])

    send_channels(1, img)
    local_part(1, img, img2)
    rho, shadow_image = collect(0, 2)
    alpha = rho / shadow_image
    receive(1, img2)
    half[...] = b_ref[...] - alpha * img[...]
    bent[...] = img[...] - alpha * img2[...]
    share(1, [
        (bent[...], half[...]), (bent[...], bent[...]),
        (b_ref[...], bent[...]), (b_ref[...], half[...]),
    ])

    send_channels(2, bent)
    local_part(2, bent, bent_img)
    tilt, square, shadow_bent, shadow_half = collect(1, 4)
    omega = tilt / square
    rho_next = shadow_half - omega * shadow_bent
    beta = rho_next / rho * (alpha / omega)
    adj_ref[...] = alpha * b_ref[...] + omega * half[...]
    res_ref[...] = half[...] - omega * bent[...]
    direc[...] = res_ref[...] + beta * (b_ref[...] - omega * img[...])
    img2[...] = bent[...] + beta * (img[...] - omega * img2[...])
    receive(2, bent_img)
    img[...] = img2[...] - omega * bent_img[...]
    share(2, [(b_ref[...], img[...])])

    send_channels(3, img)
    local_part(3, img, img2)
    (shadow_image,) = collect(2, 1)
    alpha = rho_next / shadow_image
    half[...] = res_ref[...] - alpha * img[...]
    bent[...] = bent[...] - omega * bent_img[...]
    adj_ref[...] = adj_ref[...] + alpha * direc[...]
    receive(3, img2)
    bent[...] = bent[...] - alpha * img2[...]
    share(3, [(bent[...], half[...]), (bent[...], bent[...])])
    tilt, square = collect(3, 2)
    omega = tilt / square
    adj_ref[...] = adj_ref[...] + omega * half[...]
    res_ref[...] = half[...] - omega * bent[...]

    for step in range(4):
        for j in range(4):
            @pl.when(has_target(j))
            def _():
                message(step, j).wait_send()

        def sent(i, carry):
            partial_copy(step, lax.rem(me + i, n), me).wait_send()
            return carry

        lax.fori_loop(1, n, sent, 0)


def local(blocks, couplings, cotangent):
    tiles, slots, fields, _, cells = blocks.shape
    n = lax.axis_size("row")
    far = max(2, n // 8)
    field = (tiles, fields, cells)
    f32 = jnp.float32
    vmem = pl.BlockSpec(memory_space=pltpu.VMEM)
    return pl.pallas_call(
        functools.partial(kernel, n, far),
        out_shape=(jax.ShapeDtypeStruct(field, f32), jax.ShapeDtypeStruct(field, f32)),
        in_specs=[
            pl.BlockSpec(memory_space=pl.ANY),
            pl.BlockSpec(memory_space=pltpu.SMEM),
            vmem,
        ],
        out_specs=(vmem, vmem),
        scratch_shapes=[
            pltpu.VMEM((slots, tiles, fields, fields, cells), f32),
            pltpu.VMEM((2, fields, fields, cells), f32),
        ]
        + [pltpu.VMEM(field, f32)] * 6
        + [
            pltpu.VMEM((tiles + 1, fields, cells), f32),
            pltpu.VMEM((tiles + 1, fields, cells), f32),
            pltpu.VMEM((4, 4, tiles + 1, fields, cells), f32),
            pltpu.VMEM((4, 8, cells), f32),
            pltpu.VMEM((4, n, 8, cells), f32),
            pltpu.SemaphoreType.DMA((9,)),
            pltpu.SemaphoreType.DMA((4, 4)),
            pltpu.SemaphoreType.DMA((4, 4)),
            pltpu.SemaphoreType.DMA((4, n)),
            pltpu.SemaphoreType.DMA((4, n)),
        ]
        + [pltpu.VMEM((tiles + 1, fields, cells), f32)] * 16,
        compiler_params=pltpu.CompilerParams(
            collective_id=0, has_side_effects=True, vmem_limit_bytes=40 * 1024 * 1024
        ),
        name="adjoint_solve",
    )(blocks, couplings, cotangent)


def solution(mesh):
    placed = (
        P(("grp", "row"), None, None, None, None),
        P(("grp", "row"), None),
        P(("grp", "row"), None, None),
    )
    return jax.shard_map(
        local,
        mesh=mesh,
        in_specs=placed,
        out_specs=(P(("grp", "row"), None, None), P(("grp", "row"), None, None)),
        check_vma=False,
    )
```

time: 353 us -> 55.7 us (0.16)
  blocking collectives: 159 us -> 0 us
  starting transfers between devices: 81.8 us -> 0 us
  Pallas kernels: 0 us -> 47.2 us
  local copies, waits for them, and re-layouts: 43.5 us -> 7.69 us
  other arithmetic: 32.6 us -> 0 us
  waiting for transfers between devices: 22.6 us -> 0 us
  between operations: 10.8 us -> 0.64 us
    psum x5 -> x0, blocking collectives: 159 us -> none  [the longest x2 60.9 us: local(): lax.psum((inner_sum(bent_image, half_step), inner_sum(bent_image, bent_im...]
    ppermute x30 -> x0, starting transfers between devices: 81.8 us -> none  [the longest x20 56 us: from_behind(): return lax.ppermute(array, axis, pairs)]
    pallas_call x0 -> x1, Pallas kernels: none -> 47.2 us  [local(): pl.pallas_call(functools.partial(kernel, n, far), out_shape=(jax.ShapeDty...]
    ppermute x30 -> x0, waiting for transfers between devices: 22.6 us -> none  [the longest x20 13.2 us: from_behind(): return lax.ppermute(array, axis, pairs)]
    reduce_sum x10 -> x0, other arithmetic: 17.8 us -> none  [the longest x4 13.8 us: apply_adjoint(): return jnp.sum(transposed * stacked[:, :, None], axis=(1, 3))]
    gather x20 -> x0, local copies, waits for them, and re-layouts: 16.4 us -> none  [pick_tiles(): picked = arrived[local_rows]]
    unnamed x28 -> x0, other arithmetic: 11.8 us -> none
    slice x21 -> x0, local copies, waits for them, and re-layouts: 6.4 us -> none  [the longest x9 1.91 us: after_cell(): moved = jnp.concatenate([first_cells[1:], incoming[None]], axis=0)]
  transfers between devices with their start and end apart: 30 -> 0, of which waited for: 9 -> 0; matrix products, arithmetic and copies ran while one was open for 13% -> 0% of each run, Pallas kernels for 0% -> 0%
where the time goes in v1:
time: 55.7 us; the launch traced here: 55.5 us
  Pallas kernels  47.2 us (85%)
  local copies, waits for them, and re-layouts  7.69 us (14%)
  between operations  0.64 us (1%)
    pallas_call x1, Pallas kernels, local(): pl.pallas_call(functools.partial(kernel, n, far), out_shape=(jax.ShapeDty...  47.2 us
    unnamed x3, local copies, waits for them, and re-layouts  6.37 us
    pallas_call x2, local copies, waits for them, and re-layouts, local(): pl.pallas_call(functools.partial(kernel, n, far), out_shape=(jax.ShapeDty...  1.32 us

profile of v1, /device:TPU:0, one launch (start us, length us, event | category | flops | bytes accessed | tf_op | source)
XLA Modules:
  0.0 55.5 jit_solution(8372448765730137662)
XLA Ops:
  0.6 0.8 %copy.6.coup = s32[32,4]{1,0:T(8,128)S(1)} copy(s32[32,4]{0,1:T(4,128)} %param.4) | data formatting | bytes 1024 | tf_op args[1]
  1.4 1.0 %copy.7.b_ref = f32[32,6,128]{2,1,0:T(8,128)S(1)} copy(f32[32,6,128]{2,0,1:T(8,128)} %param.5) | data formatting | bytes 196608 | tf_op args[2]
  2.3 4.7 %copy.5.blocks_hbm = f32[32,7,6,6,128]{4,3,2,1,0:T(8,128)S(1)} copy(f32[32,7,6,6,128]{4,0,3,2,1:T(8,128)} %param.3) | data formatting | bytes 8257536 | tf_op args[0]
  7.0 47.2 %adjoint_solve.1 = (f32[32,6,128]{2,1,0:T(8,128)S(1)}, f32[32,6,128]{2,1,0:T(8,128)S(1)}) custom-call(f32[32,7,6,6,128]{4,3,2,1,0:T(8,128)S(1)} %copy.5.blocks_hbm, s32[32,4]{1,0:T(8,128)S(1)} %copy.6.coup, f32[32,6,128]{2,1,0:T(8,128)S(1)} %copy.7.b_ref), custom_call_target="tpu_custom_call" | custom-call | tf_op jit(solution)/shard_map/adjoint_solve/pallas_call | solution.py:259
  54.2 0.7 %copy.8 = f32[32,6,128]{2,0,1:T(8,128)} copy(f32[32,6,128]{2,1,0:T(8,128)S(1)} %get-tuple-element.2) | data formatting | bytes 196608 | tf_op jit(solution)/shard_map/adjoint_solve/pallas_call | solution.py:259
  54.8 0.7 %copy.9 = f32[32,6,128]{2,0,1:T(8,128)} copy(f32[32,6,128]{2,1,0:T(8,128)S(1)} %get-tuple-element.3) | data formatting | bytes 196608 | tf_op jit(solution)/shard_map/adjoint_solve/pallas_call | solution.py:259

commit v2 on v1

v2 whole, which is shorter than its diff:
```python
import functools

import jax
import jax.numpy as jnp
from jax import lax
from jax.experimental import pallas as pl
from jax.experimental.pallas import tpu as pltpu
from jax.sharding import PartitionSpec as P

MESH = pl.DeviceIdType.MESH
PAIRED = (1, 0, 3, 2)
ORDER = (2, 3, 0, 1)


def kernel(
    n, far, blocks_hbm, coup, b_ref, adj_ref, res_ref,
    blk, edge_blk, origin, img, img2, bent, bent_img, direc, half,
    send, recv, red_send, red,
    load_sem, send_sem, recv_sem, red_send_sem, red_recv_sem,
):
    fields, tiles, cells = b_ref.shape
    me = lax.axis_index("row")
    offsets = (1, -1, far, -far)
    body = fields * tiles

    def load(slot):
        return pltpu.make_async_copy(blocks_hbm.at[slot], blk.at[slot], load_sem.at[slot])

    edge_loads = (
        pltpu.make_async_copy(
            blocks_hbm.at[2, :, :, pl.ds(tiles - 8, 8)], edge_blk.at[0], load_sem.at[7]
        ),
        pltpu.make_async_copy(
            blocks_hbm.at[1, :, :, pl.ds(0, 8)], edge_blk.at[1], load_sem.at[8]
        ),
    )
    load(3 + ORDER[0]).start()
    load(3 + ORDER[1]).start()
    edge_loads[0].start()
    edge_loads[1].start()
    load(3 + ORDER[2]).start()
    load(3 + ORDER[3]).start()
    for slot in (1, 2, 0):
        load(slot).start()

    barrier = pltpu.get_barrier_semaphore()

    def greet(i, carry):
        other = lax.rem(me + i, n)
        pl.semaphore_signal(barrier, inc=1, device_id={"row": other}, device_id_type=MESH)
        return carry

    lax.fori_loop(1, n, greet, 0)

    def has_target(j):
        to = me + offsets[j]
        return jnp.logical_and(to >= 0, to < n)

    def has_source(j):
        start = me - offsets[j]
        return jnp.logical_and(start >= 0, start < n)

    for j in range(4):
        @pl.when(jnp.logical_not(has_source(j)))
        def _():
            for step in range(4):
                recv[step, j] = jnp.zeros(recv.shape[2:], jnp.float32)

    on_diagonal = lax.broadcasted_iota(jnp.int32, (tiles, tiles), 0) == (
        lax.broadcasted_iota(jnp.int32, (tiles, tiles), 1)
    )
    for j in range(4):
        row = jnp.bitwise_and(coup[PAIRED[j]:PAIRED[j] + 1, :], tiles - 1)
        spread = jnp.where(on_diagonal, jnp.broadcast_to(row, (tiles, tiles)), 0)
        column = jnp.sum(spread.astype(jnp.float32), axis=1, keepdims=True)
        origin[j] = jnp.broadcast_to(column.astype(jnp.int32), (tiles, cells))

    def message(step, j):
        rows = pl.ds(0, body + 8 if j < 2 else body)
        return pltpu.make_async_remote_copy(
            src_ref=send.at[step, j, rows],
            dst_ref=recv.at[step, j, rows],
            send_sem=send_sem.at[step, j],
            recv_sem=recv_sem.at[step, j],
            device_id={"row": me + offsets[j]},
            device_id_type=MESH,
        )

    lane = lax.broadcasted_iota(jnp.int32, (8, cells), 1)
    row8 = lax.broadcasted_iota(jnp.int32, (8, cells), 0)
    first_lane = lane == 0
    last_lane = lane == cells - 1

    def product(values, block):
        out = []
        for b in range(fields):
            total = block(0, b) * values[0]
            for a in range(1, fields):
                total = total + block(a, b) * values[a]
            out.append(total)
        return out

    def send_channels(step, field):
        for j in ORDER:
            if step == 0:
                load(3 + j).wait()

            @pl.loop(0, tiles // 8, unroll=True)
            def _(chunk):
                start = pl.multiple_of(chunk * 8, 8)
                rows = pl.ds(start, 8)
                values = [field[a, rows, :] for a in range(fields)]
                moved = product(values, lambda a, b: blk[3 + j, a, b, rows, :])
                for b in range(fields):
                    send[step, j, pl.ds(pl.multiple_of(b * tiles + start, 8), 8), :] = moved[b]

            if j < 2:
                if step == 0:
                    edge_loads[j].wait()
                rows = pl.ds(tiles - 8 if j == 0 else 0, 8)
                at = 7 if j == 0 else 0
                values = [field[a, rows, :] for a in range(fields)]
                moved = product(values, lambda a, b: edge_blk[j, a, b])
                edge = jnp.zeros((8, cells), jnp.float32)
                for b in range(fields):
                    shifted = moved[b] if b == at else pltpu.roll(moved[b], (b - at) % 8, 0)
                    edge = jnp.where(row8 == b, shifted, edge)
                send[step, j, pl.ds(body, 8), :] = pltpu.roll(edge, 1 if j == 0 else cells - 1, 1)
            if step == 0 and j == ORDER[0]:
                pl.semaphore_wait(barrier, n - 1)

            @pl.when(has_target(j))
            def _():
                message(step, j).start()

    def local_part(step, field, out):
        if step == 0:
            for slot in (1, 2, 0):
                load(slot).wait()
        chunks = tiles // 8
        values = [[field[a, pl.ds(8 * c, 8), :] for a in range(fields)] for c in range(chunks)]
        for b in range(fields):
            own, left, right = [], [], []
            for c in range(chunks):
                rows = pl.ds(8 * c, 8)
                sums = []
                for slot in range(3):
                    total = blk[slot, 0, b, rows, :] * values[c][0]
                    for a in range(1, fields):
                        total = total + blk[slot, a, b, rows, :] * values[c][a]
                    sums.append(total)
                own.append(sums[0])
                left.append(pltpu.roll(sums[1], cells - 1, 1))
                right.append(pltpu.roll(sums[2], 1, 1))
            up = [pltpu.roll(x, 7, 0) for x in left]
            down = [pltpu.roll(x, 1, 0) for x in right]
            for c in range(chunks):
                after = up[c + 1] if c + 1 < chunks else jnp.zeros((8, cells), jnp.float32)
                before = down[c - 1] if c else jnp.zeros((8, cells), jnp.float32)
                after = jnp.where(row8 == 7, after, up[c])
                before = jnp.where(row8 == 0, before, down[c])
                out[b, pl.ds(8 * c, 8), :] = (
                    own[c]
                    + jnp.where(last_lane, after, left[c])
                    + jnp.where(first_lane, before, right[c])
                )

    def receive(step, out):
        chunks = tiles // 8
        for j in ORDER:
            @pl.when(has_source(j))
            def _():
                message(step, j).wait_recv()

            @pl.loop(0, fields, unroll=True)
            def _(b):
                parts = [
                    recv[step, j, pl.ds(pl.multiple_of(b * tiles + 8 * c, 8), 8), :]
                    for c in range(chunks)
                ]
                for c in range(chunks):
                    place = origin[j, pl.ds(8 * c, 8), :]
                    low = jnp.bitwise_and(place, 7)
                    high = jnp.right_shift(place, 3)
                    total = jnp.take_along_axis(parts[0], low, axis=0)
                    for k in range(1, chunks):
                        total = jnp.where(
                            high == k, jnp.take_along_axis(parts[k], low, axis=0), total
                        )
                    out[b, pl.ds(8 * c, 8), :] = out[b, pl.ds(8 * c, 8), :] + total

            if j < 2:
                edge = recv[step, j, pl.ds(body, 8), :]
                at = 0 if j == 0 else 7
                rows = pl.ds(0 if j == 0 else tiles - 8, 8)
                corner = jnp.logical_and(row8 == at, first_lane if j == 0 else last_lane)
                for b in range(fields):
                    shifted = edge if b == at else pltpu.roll(edge, (at - b) % 8, 0)
                    out[b, rows, :] = out[b, rows, :] + jnp.where(corner, shifted, 0.0)

    def partial_copy(step, other, origin):
        return pltpu.make_async_remote_copy(
            src_ref=red_send.at[step],
            dst_ref=red.at[step, origin],
            send_sem=red_send_sem.at[step, other],
            recv_sem=red_recv_sem.at[step, origin],
            device_id={"row": other},
            device_id_type=MESH,
        )

    def share(step, pairs):
        rows = [
            jnp.sum(jnp.sum(x * y, axis=0), axis=0, keepdims=True) for x, y in pairs
        ]
        rows += [jnp.zeros((8 - len(rows), cells), jnp.float32)]
        tile = jnp.concatenate(rows, axis=0)
        red_send[step] = tile
        red[step, me] = tile

        def go(i, carry):
            partial_copy(step, lax.rem(me + i, n), me).start()
            return carry

        lax.fori_loop(1, n, go, 0)

    def collect(step, count):
        def arrive(i, carry):
            other = lax.rem(me + i, n)
            partial_copy(step, other, other).wait_recv()
            return carry

        lax.fori_loop(1, n, arrive, 0)
        total = jnp.sum(jnp.sum(red[step], axis=0), axis=1, keepdims=True)
        return [total[q:q + 1] for q in range(count)]

    send_channels(0, b_ref)
    local_part(0, b_ref, img)
    receive(0, img)
    b = b_ref[...]
    share(0, [(b, b), (b, img[...])])

    send_channels(1, img)
    local_part(1, img, img2)
    rho, shadow_image = collect(0, 2)
    alpha = rho / shadow_image
    receive(1, img2)
    half[...] = b_ref[...] - alpha * img[...]
    bent[...] = img[...] - alpha * img2[...]
    share(1, [
        (bent[...], half[...]), (bent[...], bent[...]),
        (b_ref[...], bent[...]), (b_ref[...], half[...]),
    ])

    send_channels(2, bent)
    local_part(2, bent, bent_img)
    tilt, square, shadow_bent, shadow_half = collect(1, 4)
    omega = tilt / square
    rho_next = shadow_half - omega * shadow_bent
    beta = rho_next / rho * (alpha / omega)
    adj_ref[...] = alpha * b_ref[...] + omega * half[...]
    res_ref[...] = half[...] - omega * bent[...]
    direc[...] = res_ref[...] + beta * (b_ref[...] - omega * img[...])
    img2[...] = bent[...] + beta * (img[...] - omega * img2[...])
    receive(2, bent_img)
    img[...] = img2[...] - omega * bent_img[...]
    share(2, [(b_ref[...], img[...])])

    send_channels(3, img)
    local_part(3, img, img2)
    (shadow_image,) = collect(2, 1)
    alpha = rho_next / shadow_image
    half[...] = res_ref[...] - alpha * img[...]
    bent[...] = bent[...] - omega * bent_img[...]
    adj_ref[...] = adj_ref[...] + alpha * direc[...]
    receive(3, img2)
    bent[...] = bent[...] - alpha * img2[...]
    share(3, [(bent[...], half[...]), (bent[...], bent[...])])
    tilt, square = collect(3, 2)
    omega = tilt / square
    adj_ref[...] = adj_ref[...] + omega * half[...]
    res_ref[...] = half[...] - omega * bent[...]

    for step in range(4):
        for j in range(4):
            @pl.when(has_target(j))
            def _():
                message(step, j).wait_send()

        def sent(i, carry):
            partial_copy(step, lax.rem(me + i, n), me).wait_send()
            return carry

        lax.fori_loop(1, n, sent, 0)


def local(blocks, couplings, cotangent):
    tiles, slots, fields, _, cells = blocks.shape
    n = lax.axis_size("row")
    far = max(2, n // 8)
    field = (fields, tiles, cells)
    f32 = jnp.float32
    vmem = pl.BlockSpec(memory_space=pltpu.VMEM)
    adjoint, residual = pl.pallas_call(
        functools.partial(kernel, n, far),
        out_shape=(jax.ShapeDtypeStruct(field, f32), jax.ShapeDtypeStruct(field, f32)),
        in_specs=[pl.BlockSpec(memory_space=pl.ANY), vmem, vmem],
        out_specs=(vmem, vmem),
        scratch_shapes=[
            pltpu.VMEM((slots, fields, fields, tiles, cells), f32),
            pltpu.VMEM((2, fields, fields, 8, cells), f32),
            pltpu.VMEM((4, tiles, cells), jnp.int32),
        ]
        + [pltpu.VMEM(field, f32)] * 6
        + [
            pltpu.VMEM((4, 4, fields * tiles + 8, cells), f32),
            pltpu.VMEM((4, 4, fields * tiles + 8, cells), f32),
            pltpu.VMEM((4, 8, cells), f32),
            pltpu.VMEM((4, n, 8, cells), f32),
            pltpu.SemaphoreType.DMA((9,)),
            pltpu.SemaphoreType.DMA((4, 4)),
            pltpu.SemaphoreType.DMA((4, 4)),
            pltpu.SemaphoreType.DMA((4, n)),
            pltpu.SemaphoreType.DMA((4, n)),
        ],
        compiler_params=pltpu.CompilerParams(
            collective_id=0, has_side_effects=True, vmem_limit_bytes=40 * 1024 * 1024
        ),
        name="adjoint_solve",
    )(
        jnp.transpose(blocks, (1, 2, 3, 0, 4)),
        jnp.transpose(couplings),
        jnp.transpose(cotangent, (1, 0, 2)),
    )
    return jnp.transpose(adjoint, (1, 0, 2)), jnp.transpose(residual, (1, 0, 2))


def solution(mesh):
    placed = (
        P(("grp", "row"), None, None, None, None),
        P(("grp", "row"), None),
        P(("grp", "row"), None, None),
    )
    return jax.shard_map(
        local,
        mesh=mesh,
        in_specs=placed,
        out_specs=(P(("grp", "row"), None, None), P(("grp", "row"), None, None)),
        check_vma=False,
    )
```

time: 55.7 us -> 51.9 us (0.932)
  local copies, waits for them, and re-layouts: 7.69 us -> 5.02 us
  Pallas kernels: 47.2 us -> 46 us
    unnamed x3 -> x8, local copies, waits for them, and re-layouts: 6.37 us -> 5.02 us
    pallas_call x2 -> x0, local copies, waits for them, and re-layouts: 1.32 us -> none  [local(): pl.pallas_call(functools.partial(kernel, n, far), out_shape=(jax.ShapeDty...]
    pallas_call x1, Pallas kernels: 47.2 us -> 46 us  [local(): pl.pallas_call(functools.partial(kernel, n, far), out_shape=(jax.ShapeDty...]
where the time goes in v2:
time: 51.9 us; the launch traced here: 51.6 us
  Pallas kernels  46 us (89%)
  local copies, waits for them, and re-layouts  5.02 us (10%)
  between operations  0.65 us (1%)
    pallas_call x1, Pallas kernels, local(): pl.pallas_call(functools.partial(kernel, n, far), out_shape=(jax.ShapeDty...  46 us
    unnamed x8, local copies, waits for them, and re-layouts  5.02 us

profile of v2, /device:TPU:0, one launch (start us, length us, event | category | flops | bytes accessed | tf_op | source)
XLA Modules:
  0.0 51.6 jit_solution(6716086109231282792)
XLA Ops:
  0.6 0.0 copy-start
  0.6 2.2 %copy-done = f32[32,7,6,6,128]{4,0,3,2,1:T(8,128)S(1)} copy-done((f32[32,7,6,6,128]{4,0,3,2,1:T(8,128)S(1)}, f32[32,7,6,6,128]{4,0,3,2,1:T(8,128)}, u32[]{:S(2)}) %copy-start) | copy-done | bytes 4128792
  2.8 0.0 copy-start.1
  2.8 0.9 %copy-done.1 = f32[32,6,128]{2,0,1:T(8,128)S(1)} copy-done((f32[32,6,128]{2,0,1:T(8,128)S(1)}, f32[32,6,128]{2,0,1:T(8,128)}, u32[]{:S(2)}) %copy-start.1) | copy-done | bytes 98328
  3.7 0.0 copy-start.2
  3.7 0.7 %copy-done.2 = s32[32,4]{0,1:T(4,128)S(1)} copy-done((s32[32,4]{0,1:T(4,128)S(1)}, s32[32,4]{0,1:T(4,128)}, u32[]{:S(2)}) %copy-start.2) | copy-done | bytes 536
  4.4 46.0 %adjoint_solve.1 = (f32[6,32,128]{2,1,0:T(8,128)S(1)}, f32[6,32,128]{2,1,0:T(8,128)S(1)}) custom-call(f32[7,6,6,32,128]{4,3,2,1,0:T(8,128)S(1)} %bitcast.5, s32[4,32]{1,0:T(4,128)S(1)} %bitcast.9, f32[6,32,128]{2,1,0:T(8,128)S(1)} %bitcast.8), custom_call_target="tpu_custom_call" | custom-call | tf_op jit(solution)/shard_map/adjoint_solve/pallas_call | solution.py:303
  50.4 0.6 %copy.7 = f32[32,6,128]{2,0,1:T(8,128)} copy(f32[32,6,128]{2,0,1:T(8,128)S(1)} %bitcast.7) | data formatting | bytes 196608
  51.0 0.6 %copy.8 = f32[32,6,128]{2,0,1:T(8,128)} copy(f32[32,6,128]{2,0,1:T(8,128)S(1)} %bitcast.6) | data formatting | bytes 196608
Async XLA Ops:
  0.6 2.2 %copy-start = (f32[32,7,6,6,128]{4,0,3,2,1:T(8,128)S(1)}, f32[32,7,6,6,128]{4,0,3,2,1:T(8,128)}, u32[]{:S(2)}) copy-start(f32[32,7,6,6,128]{4,0,3,2,1:T(8,128)} %param.3) | copy-start | bytes 12386308
  2.8 0.9 %copy-start.1 = (f32[32,6,128]{2,0,1:T(8,128)S(1)}, f32[32,6,128]{2,0,1:T(8,128)}, u32[]{:S(2)}) copy-start(f32[32,6,128]{2,0,1:T(8,128)} %param.5) | copy-start | bytes 294916
  3.7 0.7 %copy-start.2 = (s32[32,4]{0,1:T(4,128)S(1)}, s32[32,4]{0,1:T(4,128)}, u32[]{:S(2)}) copy-start(s32[32,4]{0,1:T(4,128)} %param.4) | copy-start | bytes 1540

commit v3 on v2

--- a/solution.py
+++ b/solution.py
@@ -9,19 +9,21 @@
 
 MESH = pl.DeviceIdType.MESH
 PAIRED = (1, 0, 3, 2)
+SUMS = (2, 4, 1, 2)
 ORDER = (2, 3, 0, 1)
 
 
 def kernel(
     n, far, blocks_hbm, coup, b_ref, adj_ref, res_ref,
     blk, edge_blk, origin, img, img2, bent, bent_img, direc, half,
-    send, recv, red_send, red,
-    load_sem, send_sem, recv_sem, red_send_sem, red_recv_sem,
+    send, recv, load_sem, send_sem, recv_sem, red_send_sem, red_recv_sem, *sums
 ):
+    red_send, red = sums[:4], sums[4:]
     fields, tiles, cells = b_ref.shape
     me = lax.axis_index("row")
     offsets = (1, -1, far, -far)
     body = fields * tiles
+    paired = far == 2 and n % 2 == 0
 
     def load(slot):
         return pltpu.make_async_copy(blocks_hbm.at[slot], blk.at[slot], load_sem.at[slot])
@@ -34,12 +36,14 @@
             blocks_hbm.at[1, :, :, pl.ds(0, 8)], edge_blk.at[1], load_sem.at[8]
         ),
     )
-    load(3 + ORDER[0]).start()
-    load(3 + ORDER[1]).start()
+    parity = lax.rem(me, 2)
+    order = (2 + parity, 3 - parity, 1 - parity, parity) if paired else ORDER
+    load(3 + order[0]).start()
+    load(3 + order[1]).start()
     edge_loads[0].start()
     edge_loads[1].start()
-    load(3 + ORDER[2]).start()
-    load(3 + ORDER[3]).start()
+    load(3 + order[2]).start()
+    load(3 + order[3]).start()
     for slot in (1, 2, 0):
         load(slot).start()
 
@@ -60,20 +64,40 @@
         start = me - offsets[j]
         return jnp.logical_and(start >= 0, start < n)
 
-    for j in range(4):
-        @pl.when(jnp.logical_not(has_source(j)))
-        def _():
-            for step in range(4):
-                recv[step, j] = jnp.zeros(recv.shape[2:], jnp.float32)
-
-    on_diagonal = lax.broadcasted_iota(jnp.int32, (tiles, tiles), 0) == (
-        lax.broadcasted_iota(jnp.int32, (tiles, tiles), 1)
-    )
-    for j in range(4):
-        row = jnp.bitwise_and(coup[PAIRED[j]:PAIRED[j] + 1, :], tiles - 1)
-        spread = jnp.where(on_diagonal, jnp.broadcast_to(row, (tiles, tiles)), 0)
+    def clear(kind):
+        for step in range(4):
+            recv[step, kind] = jnp.zeros(recv.shape[2:], jnp.float32)
+
+    if paired:
+        at_end = lax.rem(me, 2) == 0
+        sign0 = jnp.where(at_end, -1, 1)
+        no_outward = jnp.logical_or(me + sign0 < 0, me + sign0 >= n)
+        no_inward = jnp.logical_or(me - 2 * sign0 < 0, me - 2 * sign0 >= n)
+        pl.when(no_outward)(lambda: clear(3))
+        pl.when(no_inward)(lambda: clear(1))
+    else:
+        for j in range(4):
+            pl.when(jnp.logical_not(has_source(j)))(functools.partial(clear, j))
+
+    down = lax.broadcasted_iota(jnp.int32, (tiles, tiles), 0)
+    across = lax.broadcasted_iota(jnp.int32, (tiles, tiles), 1)
+
+    def column_of(row, inverse):
+        row = jnp.broadcast_to(jnp.bitwise_and(row, tiles - 1), (tiles, tiles))
+        spread = jnp.where(row == down, across, 0) if inverse else jnp.where(down == across, row, 0)
         column = jnp.sum(spread.astype(jnp.float32), axis=1, keepdims=True)
-        origin[j] = jnp.broadcast_to(column.astype(jnp.int32), (tiles, cells))
+        return jnp.broadcast_to(column.astype(jnp.int32), (tiles, cells))
+
+    if paired:
+        even = lax.rem(me, 2) == 0
+        pair_rows = [jnp.where(even, coup[k:k + 1, :], coup[m:m + 1, :]) for k, m in ((0, 1), (2, 3), (1, 0))]
+        origin[0] = column_of(pair_rows[0], False)
+        origin[1] = column_of(pair_rows[1], False)
+        origin[2] = column_of(pair_rows[1], True)
+        origin[3] = column_of(pair_rows[2], True)
+    else:
+        for j in range(4):
+            origin[j] = column_of(coup[PAIRED[j]:PAIRED[j] + 1, :], False)
 
     def message(step, j):
         rows = pl.ds(0, body + 8 if j < 2 else body)
@@ -198,12 +222,145 @@
                     shifted = edge if b == at else pltpu.roll(edge, (at - b) % 8, 0)
                     out[b, rows, :] = out[b, rows, :] + jnp.where(corner, shifted, 0.0)
 
-    def partial_copy(step, other, origin):
+    core = lax.rem(me, 2)
+    sign = 2 * core - 1
+    outward = jnp.logical_and(me + sign >= 0, me + sign < n)
+    inward = jnp.logical_and(me - 2 * sign >= 0, me - 2 * sign < n)
+    NEAR, SOLO, RELAY, MERGED = range(4)
+    reach = (-sign, 2 * sign, -sign, sign)
+    channel = (core, 3 - core, 2 + core, 1 - core)
+
+    def pair_message(step, kind):
+        rows = pl.ds(0, body + 8 if kind in (NEAR, MERGED) else body)
         return pltpu.make_async_remote_copy(
-            src_ref=red_send.at[step],
-            dst_ref=red.at[step, origin],
+            src_ref=send.at[step, kind, rows],
+            dst_ref=recv.at[step, kind, rows],
+            send_sem=send_sem.at[step, kind],
+            recv_sem=recv_sem.at[step, kind],
+            device_id={"row": me + reach[kind]},
+            device_id_type=MESH,
+        )
+
+    def permuted(parts, which):
+        out = []
+        for c in range(len(parts)):
+            place = origin[which, pl.ds(8 * c, 8), :]
+            low = jnp.bitwise_and(place, 7)
+            high = jnp.right_shift(place, 3)
+            total = jnp.take_along_axis(parts[0], low, axis=0)
+            for k in range(1, len(parts)):
+                total = jnp.where(high == k, jnp.take_along_axis(parts[k], low, axis=0), total)
+            out.append(total)
+        return out
+
+    def fill(step, field, kind):
+        chunks = tiles // 8
+        slot = 3 + channel[kind]
+        for b in range(fields):
+            parts = []
+            for c in range(chunks):
+                rows = pl.ds(8 * c, 8)
+                total = blk[slot, 0, b, rows, :] * field[0, rows, :]
+                for a in range(1, fields):
+                    total = total + blk[slot, a, b, rows, :] * field[a, rows, :]
+                parts.append(total)
+            if kind in (RELAY, MERGED):
+                parts = permuted(parts, kind)
+            for c in range(chunks):
+                send[step, kind, pl.ds(b * tiles + 8 * c, 8), :] = parts[c]
+
+    def edge_row(field, which):
+        rows = pl.ds(tiles - 8 if which == 0 else 0, 8)
+        at = 7 if which == 0 else 0
+        values = [field[a, rows, :] for a in range(fields)]
+        moved = product(values, lambda a, b: edge_blk[which, a, b])
+        edge = jnp.zeros((8, cells), jnp.float32)
+        for b in range(fields):
+            shifted = moved[b] if b == at else pltpu.roll(moved[b], (b - at) % 8, 0)
+            edge = jnp.where(row8 == b, shifted, edge)
+        return pltpu.roll(edge, 1 if which == 0 else cells - 1, 1)
+
+    def send_first(step, field):
+        if step == 0:
+            load(3 + channel[RELAY]).wait()
+        fill(step, field, RELAY)
+        if step == 0:
+            pl.semaphore_wait(barrier, n - 1)
+
+        @pl.when(inward)
+        def _():
+            pair_message(step, RELAY).start()
+
+        if step == 0:
+            load(3 + channel[SOLO]).wait()
+        fill(step, field, SOLO)
+
+        @pl.when(outward)
+        def _():
+            pair_message(step, SOLO).start()
+
+        if step == 0:
+            for which in range(2):
+                edge_loads[which].wait()
+        ahead, behind = edge_row(field, 0), edge_row(field, 1)
+        first = core == 0
+        send[step, NEAR, pl.ds(body, 8), :] = jnp.where(first, ahead, behind)
+        send[step, MERGED, pl.ds(body, 8), :] = jnp.where(first, behind, ahead)
+        if step == 0:
+            load(3 + channel[MERGED]).wait()
+        fill(step, field, MERGED)
+        if step == 0:
+            load(3 + channel[NEAR]).wait()
+        fill(step, field, NEAR)
+        pair_message(step, NEAR).start()
+
+        @pl.when(outward)
+        def _():
+            pair_message(step, RELAY).wait_recv()
+            send[step, MERGED, pl.ds(0, body), :] = (
+                send[step, MERGED, pl.ds(0, body), :] + recv[step, RELAY, pl.ds(0, body), :]
+            )
+            pair_message(step, MERGED).start()
+
+    def pair_receive(step, out):
+        chunks = tiles // 8
+        for kind in (NEAR, SOLO, MERGED):
+            if kind == NEAR:
+                pair_message(step, kind).wait_recv()
+            else:
+                @pl.when(inward if kind == SOLO else outward)
+                def _():
+                    pair_message(step, kind).wait_recv()
+
+            for b in range(fields):
+                parts = [
+                    recv[step, kind, pl.ds(b * tiles + 8 * c, 8), :] for c in range(chunks)
+                ]
+                if kind != MERGED:
+                    parts = permuted(parts, kind)
+                for c in range(chunks):
+                    rows = pl.ds(8 * c, 8)
+                    out[b, rows, :] = out[b, rows, :] + parts[c]
+        near, merged = recv[step, NEAR, pl.ds(body, 8), :], recv[step, MERGED, pl.ds(body, 8), :]
+        first = core == 0
+        for j in range(2):
+            edge = jnp.where(first, merged, near) if j == 0 else jnp.where(first, near, merged)
+            at = 0 if j == 0 else 7
+            rows = pl.ds(0 if j == 0 else tiles - 8, 8)
+            corner = jnp.logical_and(row8 == at, first_lane if j == 0 else last_lane)
+            for b in range(fields):
+                shifted = edge if b == at else pltpu.roll(edge, (at - b) % 8, 0)
+                out[b, rows, :] = out[b, rows, :] + jnp.where(corner, shifted, 0.0)
+
+    if paired:
+        send_channels, receive = send_first, pair_receive
+
+    def partial_copy(step, other, source):
+        return pltpu.make_async_remote_copy(
+            src_ref=red_send[step],
+            dst_ref=red[step].at[source],
             send_sem=red_send_sem.at[step, other],
-            recv_sem=red_recv_sem.at[step, origin],
+            recv_sem=red_recv_sem.at[step, source],
             device_id={"row": other},
             device_id_type=MESH,
         )
@@ -212,16 +369,15 @@
         rows = [
             jnp.sum(jnp.sum(x * y, axis=0), axis=0, keepdims=True) for x, y in pairs
         ]
-        rows += [jnp.zeros((8 - len(rows), cells), jnp.float32)]
-        tile = jnp.concatenate(rows, axis=0)
-        red_send[step] = tile
-        red[step, me] = tile
+        row = jnp.concatenate(rows, axis=0)
+        red_send[step][...] = row
+        red[step][me] = row
 
         def go(i, carry):
             partial_copy(step, lax.rem(me + i, n), me).start()
             return carry
 
-        lax.fori_loop(1, n, go, 0)
+        lax.fori_loop(1, n, go, 0, unroll=True)
 
     def collect(step, count):
         def arrive(i, carry):
@@ -229,8 +385,8 @@
             partial_copy(step, other, other).wait_recv()
             return carry
 
-        lax.fori_loop(1, n, arrive, 0)
-        total = jnp.sum(jnp.sum(red[step], axis=0), axis=1, keepdims=True)
+        lax.fori_loop(1, n, arrive, 0, unroll=True)
+        total = jnp.sum(jnp.sum(red[step][...], axis=0), axis=1, keepdims=True)
         return [total[q:q + 1] for q in range(count)]
 
     send_channels(0, b_ref)
@@ -281,10 +437,22 @@
     res_ref[...] = half[...] - omega * bent[...]
 
     for step in range(4):
-        for j in range(4):
-            @pl.when(has_target(j))
+        if paired:
+            pair_message(step, NEAR).wait_send()
+
+            @pl.when(inward)
             def _():
-                message(step, j).wait_send()
+                pair_message(step, RELAY).wait_send()
+
+            @pl.when(outward)
+            def _():
+                pair_message(step, SOLO).wait_send()
+                pair_message(step, MERGED).wait_send()
+        else:
+            for j in range(4):
+                @pl.when(has_target(j))
+                def _():
+                    message(step, j).wait_send()
 
         def sent(i, carry):
             partial_copy(step, lax.rem(me + i, n), me).wait_send()
@@ -303,7 +471,7 @@
     adjoint, residual = pl.pallas_call(
         functools.partial(kernel, n, far),
         out_shape=(jax.ShapeDtypeStruct(field, f32), jax.ShapeDtypeStruct(field, f32)),
-        in_specs=[pl.BlockSpec(memory_space=pl.ANY), vmem, vmem],
+        in_specs=[pl.BlockSpec(memory_space=pltpu.HBM), vmem, vmem],
         out_specs=(vmem, vmem),
         scratch_shapes=[
             pltpu.VMEM((slots, fields, fields, tiles, cells), f32),
@@ -314,16 +482,16 @@
         + [
             pltpu.VMEM((4, 4, fields * tiles + 8, cells), f32),
             pltpu.VMEM((4, 4, fields * tiles + 8, cells), f32),
-            pltpu.VMEM((4, 8, cells), f32),
-            pltpu.VMEM((4, n, 8, cells), f32),
             pltpu.SemaphoreType.DMA((9,)),
             pltpu.SemaphoreType.DMA((4, 4)),
             pltpu.SemaphoreType.DMA((4, 4)),
             pltpu.SemaphoreType.DMA((4, n)),
             pltpu.SemaphoreType.DMA((4, n)),
-        ],
+        ]
+        + [pltpu.VMEM((count, cells), f32) for count in SUMS]
+        + [pltpu.VMEM((n, count, cells), f32) for count in SUMS],
         compiler_params=pltpu.CompilerParams(
-            collective_id=0, has_side_effects=True, vmem_limit_bytes=40 * 1024 * 1024
+            collective_id=0, has_side_effects=True, vmem_limit_bytes=60 * 1024 * 1024
         ),
         name="adjoint_solve",
     )(

time: 51.9 us -> 42.2 us (0.81)
  Pallas kernels: 46 us -> 38.2 us
  local copies, waits for them, and re-layouts: 5.02 us -> 3.08 us
    pallas_call x1, Pallas kernels: 46 us -> 38.2 us  [local(): pl.pallas_call(functools.partial(kernel, n, far), out_shape=(jax.ShapeDty...]
    unnamed x8 -> x2, local copies, waits for them, and re-layouts: 5.02 us -> 3.08 us
where the time goes in v3:
time: 42.2 us; the launch traced here: 41.9 us
  Pallas kernels  38.2 us (91%)
  local copies, waits for them, and re-layouts  3.08 us (7%)
  between operations  0.64 us (2%)
    pallas_call x1, Pallas kernels, local(): pl.pallas_call(functools.partial(kernel, n, far), out_shape=(jax.ShapeDty...  38.2 us
    unnamed x2, local copies, waits for them, and re-layouts  3.08 us

profile of v3, /device:TPU:0, one launch (start us, length us, event | category | flops | bytes accessed | tf_op | source)
XLA Modules:
  0.0 41.9 jit_solution(15163595509436015037)
XLA Ops:
  0.6 38.2 %adjoint_solve.1 = (f32[6,32,128]{2,1,0:T(8,128)}, f32[6,32,128]{2,1,0:T(8,128)}) custom-call(f32[7,6,6,32,128]{4,3,2,1,0:T(8,128)} %bitcast.5, s32[4,32]{1,0:T(4,128)} %bitcast.9, f32[6,32,128]{2,1,0:T(8,128)} %bitcast.8), custom_call_target="tpu_custom_call" | custom-call | tf_op jit(solution)/shard_map/adjoint_solve/pallas_call | solution.py:471
  38.9 1.5 %copy.7 = f32[32,6,128]{2,0,1:T(8,128)} copy(f32[32,6,128]{2,0,1:T(8,128)} %bitcast.7) | data formatting | bytes 196608
  40.4 1.5 %copy.8 = f32[32,6,128]{2,0,1:T(8,128)} copy(f32[32,6,128]{2,0,1:T(8,128)} %bitcast.6) | data formatting | bytes 196608

commit v4 on v3

--- a/solution.py
+++ b/solution.py
@@ -14,11 +14,14 @@
 
 
 def kernel(
-    n, far, blocks_hbm, coup, b_ref, adj_ref, res_ref,
+    n, far, group, blocks_hbm, coup_hbm, b_hbm, adj_ref, res_ref,
+    coup, b_ref,
     blk, edge_blk, origin, img, img2, bent, bent_img, direc, half,
-    send, recv, load_sem, send_sem, recv_sem, red_send_sem, red_recv_sem, *sums
+    send, recv, load_sem, send_sem, recv_sem,
+    first_send_sem, first_recv_sem, second_send_sem, second_recv_sem, *sums
 ):
-    red_send, red = sums[:4], sums[4:]
+    first_sems = (first_send_sem, first_recv_sem)
+    second_sems = (second_send_sem, second_recv_sem)
     fields, tiles, cells = b_ref.shape
     me = lax.axis_index("row")
     offsets = (1, -1, far, -far)
@@ -36,6 +39,10 @@
             blocks_hbm.at[1, :, :, pl.ds(0, 8)], edge_blk.at[1], load_sem.at[8]
         ),
     )
+    b_load = pltpu.make_async_copy(b_hbm, b_ref, load_sem.at[9])
+    coup_load = pltpu.make_async_copy(coup_hbm, coup, load_sem.at[10])
+    coup_load.start()
+    b_load.start()
     parity = lax.rem(me, 2)
     order = (2 + parity, 3 - parity, 1 - parity, parity) if paired else ORDER
     load(3 + order[0]).start()
@@ -88,6 +95,7 @@
         column = jnp.sum(spread.astype(jnp.float32), axis=1, keepdims=True)
         return jnp.broadcast_to(column.astype(jnp.int32), (tiles, cells))
 
+    coup_load.wait()
     if paired:
         even = lax.rem(me, 2) == 0
         pair_rows = [jnp.where(even, coup[k:k + 1, :], coup[m:m + 1, :]) for k, m in ((0, 1), (2, 3), (1, 0))]
@@ -314,6 +322,7 @@
         fill(step, field, NEAR)
         pair_message(step, NEAR).start()
 
+    def send_merged(step):
         @pl.when(outward)
         def _():
             pair_message(step, RELAY).wait_recv()
@@ -353,15 +362,30 @@
                 out[b, rows, :] = out[b, rows, :] + jnp.where(corner, shifted, 0.0)
 
     if paired:
-        send_channels, receive = send_first, pair_receive
-
-    def partial_copy(step, other, source):
+        send_channels, send_rest, receive = send_first, send_merged, pair_receive
+    else:
+        send_rest = lambda step: None
+
+    rank, team = lax.rem(me, group), me // group
+    first_send, first_at, second_send, second_at = sums[:4], sums[4:8], sums[8:12], sums[12:]
+
+    def first_copy(step, i, source):
         return pltpu.make_async_remote_copy(
-            src_ref=red_send[step],
-            dst_ref=red[step].at[source],
-            send_sem=red_send_sem.at[step, other],
-            recv_sem=red_recv_sem.at[step, source],
-            device_id={"row": other},
+            src_ref=first_send[step],
+            dst_ref=first_at[step].at[source],
+            send_sem=first_sems[0].at[step, i],
+            recv_sem=first_sems[1].at[step, source],
+            device_id={"row": team * group + lax.rem(rank + i, group)},
+            device_id_type=MESH,
+        )
+
+    def second_copy(step, i, source):
+        return pltpu.make_async_remote_copy(
+            src_ref=second_send[step],
+            dst_ref=second_at[step].at[source],
+            send_sem=second_sems[0].at[step, i],
+            recv_sem=second_sems[1].at[step, source],
+            device_id={"row": lax.rem(me + i * group, n)},
             device_id_type=MESH,
         )
 
@@ -370,33 +394,38 @@
             jnp.sum(jnp.sum(x * y, axis=0), axis=0, keepdims=True) for x, y in pairs
         ]
         row = jnp.concatenate(rows, axis=0)
-        red_send[step][...] = row
-        red[step][me] = row
-
-        def go(i, carry):
-            partial_copy(step, lax.rem(me + i, n), me).start()
-            return carry
-
-        lax.fori_loop(1, n, go, 0, unroll=True)
+        first_send[step][...] = row
+        first_at[step][rank] = row
+        for i in range(1, group):
+            first_copy(step, i, rank).start()
+
+    def pass_on(step):
+        for i in range(1, group):
+            first_copy(step, i, lax.rem(rank + i, group)).wait_recv()
+        row = jnp.sum(first_at[step][...], axis=0)
+        second_send[step][...] = row
+        second_at[step][team] = row
+        for i in range(1, n // group):
+            second_copy(step, i, team).start()
 
     def collect(step, count):
-        def arrive(i, carry):
-            other = lax.rem(me + i, n)
-            partial_copy(step, other, other).wait_recv()
-            return carry
-
-        lax.fori_loop(1, n, arrive, 0, unroll=True)
-        total = jnp.sum(jnp.sum(red[step][...], axis=0), axis=1, keepdims=True)
+        for i in range(1, n // group):
+            second_copy(step, i, lax.rem(team + i, n // group)).wait_recv()
+        total = jnp.sum(jnp.sum(second_at[step][...], axis=0), axis=1, keepdims=True)
         return [total[q:q + 1] for q in range(count)]
 
+    b_load.wait()
     send_channels(0, b_ref)
     local_part(0, b_ref, img)
+    send_rest(0)
     receive(0, img)
     b = b_ref[...]
     share(0, [(b, b), (b, img[...])])
 
     send_channels(1, img)
     local_part(1, img, img2)
+    send_rest(1)
+    pass_on(0)
     rho, shadow_image = collect(0, 2)
     alpha = rho / shadow_image
     receive(1, img2)
@@ -409,6 +438,8 @@
 
     send_channels(2, bent)
     local_part(2, bent, bent_img)
+    send_rest(2)
+    pass_on(1)
     tilt, square, shadow_bent, shadow_half = collect(1, 4)
     omega = tilt / square
     rho_next = shadow_half - omega * shadow_bent
@@ -423,6 +454,8 @@
 
     send_channels(3, img)
     local_part(3, img, img2)
+    send_rest(3)
+    pass_on(2)
     (shadow_image,) = collect(2, 1)
     alpha = rho_next / shadow_image
     half[...] = res_ref[...] - alpha * img[...]
@@ -431,6 +464,7 @@
     receive(3, img2)
     bent[...] = bent[...] - alpha * img2[...]
     share(3, [(bent[...], half[...]), (bent[...], bent[...])])
+    pass_on(3)
     tilt, square = collect(3, 2)
     omega = tilt / square
     adj_ref[...] = adj_ref[...] + omega * half[...]
@@ -454,26 +488,28 @@
                 def _():
                     message(step, j).wait_send()
 
-        def sent(i, carry):
-            partial_copy(step, lax.rem(me + i, n), me).wait_send()
-            return carry
-
-        lax.fori_loop(1, n, sent, 0)
+        for i in range(1, group):
+            first_copy(step, i, rank).wait_send()
+        for i in range(1, n // group):
+            second_copy(step, i, team).wait_send()
 
 
 def local(blocks, couplings, cotangent):
     tiles, slots, fields, _, cells = blocks.shape
     n = lax.axis_size("row")
     far = max(2, n // 8)
+    group = n
     field = (fields, tiles, cells)
     f32 = jnp.float32
     vmem = pl.BlockSpec(memory_space=pltpu.VMEM)
     adjoint, residual = pl.pallas_call(
-        functools.partial(kernel, n, far),
+        functools.partial(kernel, n, far, group),
         out_shape=(jax.ShapeDtypeStruct(field, f32), jax.ShapeDtypeStruct(field, f32)),
-        in_specs=[pl.BlockSpec(memory_space=pltpu.HBM), vmem, vmem],
+        in_specs=[pl.BlockSpec(memory_space=pltpu.HBM)] * 3,
         out_specs=(vmem, vmem),
         scratch_shapes=[
+            pltpu.VMEM((4, tiles), jnp.int32),
+            pltpu.VMEM(field, f32),
             pltpu.VMEM((slots, fields, fields, tiles, cells), f32),
             pltpu.VMEM((2, fields, fields, 8, cells), f32),
             pltpu.VMEM((4, tiles, cells), jnp.int32),
@@ -482,16 +518,20 @@
         + [
             pltpu.VMEM((4, 4, fields * tiles + 8, cells), f32),
             pltpu.VMEM((4, 4, fields * tiles + 8, cells), f32),
-            pltpu.SemaphoreType.DMA((9,)),
+            pltpu.SemaphoreType.DMA((11,)),
             pltpu.SemaphoreType.DMA((4, 4)),
             pltpu.SemaphoreType.DMA((4, 4)),
-            pltpu.SemaphoreType.DMA((4, n)),
-            pltpu.SemaphoreType.DMA((4, n)),
+            pltpu.SemaphoreType.DMA((4, group)),
+            pltpu.SemaphoreType.DMA((4, group)),
+            pltpu.SemaphoreType.DMA((4, n // group)),
+            pltpu.SemaphoreType.DMA((4, n // group)),
         ]
         + [pltpu.VMEM((count, cells), f32) for count in SUMS]
-        + [pltpu.VMEM((n, count, cells), f32) for count in SUMS],
+        + [pltpu.VMEM((group, count, cells), f32) for count in SUMS]
+        + [pltpu.VMEM((count, cells), f32) for count in SUMS]
+        + [pltpu.VMEM((n // group, count, cells), f32) for count in SUMS],
         compiler_params=pltpu.CompilerParams(
-            collective_id=0, has_side_effects=True, vmem_limit_bytes=60 * 1024 * 1024
+            collective_id=0, has_side_effects=True, vmem_limit_bytes=50 * 1024 * 1024
         ),
         name="adjoint_solve",
     )(

time: 42.2 us -> 40 us (0.948)
  Pallas kernels: 38.2 us -> 36.3 us
    pallas_call x1, Pallas kernels: 38.2 us -> 36.3 us  [local(): pl.pallas_call(functools.partial(kernel, n, far, group), out_shape=(jax.S...]
    unnamed x2 -> x6, local copies, waits for them, and re-layouts: 3.08 us -> 2.85 us
where the time goes in v4:
time: 40 us; the launch traced here: 39.8 us
  Pallas kernels  36.3 us (91%)
  local copies, waits for them, and re-layouts  2.85 us (7%)
  between operations  0.65 us (2%)
    pallas_call x1, Pallas kernels, local(): pl.pallas_call(functools.partial(kernel, n, far, group), out_shape=(jax.S...  36.3 us
    unnamed x6, local copies, waits for them, and re-layouts  2.85 us

profile of v4, /device:TPU:0, one launch (start us, length us, event | category | flops | bytes accessed | tf_op | source)
XLA Modules:
  0.0 39.8 jit_solution(29388199823630118)
XLA Ops:
  0.6 0.0 copy-start
  0.6 0.9 %copy-done = f32[32,6,128]{2,0,1:T(8,128)S(1)} copy-done((f32[32,6,128]{2,0,1:T(8,128)S(1)}, f32[32,6,128]{2,0,1:T(8,128)}, u32[]{:S(2)}) %copy-start) | copy-done | bytes 98328
  1.5 0.0 copy-start.1
  1.5 0.7 %copy-done.1 = s32[32,4]{0,1:T(4,128)S(1)} copy-done((s32[32,4]{0,1:T(4,128)S(1)}, s32[32,4]{0,1:T(4,128)}, u32[]{:S(2)}) %copy-start.1) | copy-done | bytes 536
  2.2 36.3 %adjoint_solve.1 = (f32[6,32,128]{2,1,0:T(8,128)S(1)}, f32[6,32,128]{2,1,0:T(8,128)S(1)}) custom-call(f32[7,6,6,32,128]{4,3,2,1,0:T(8,128)} %bitcast.9, s32[4,32]{1,0:T(4,128)S(1)} %bitcast.8, f32[6,32,128]{2,1,0:T(8,128)S(1)} %bitcast.7), custom_call_target="tpu_custom_call" | custom-call | tf_op jit(solution)/shard_map/adjoint_solve/pallas_call | solution.py:505
  38.5 0.6 %copy.7 = f32[32,6,128]{2,0,1:T(8,128)} copy(f32[32,6,128]{2,0,1:T(8,128)S(1)} %bitcast.6) | data formatting | bytes 196608
  39.1 0.6 %copy.8 = f32[32,6,128]{2,0,1:T(8,128)} copy(f32[32,6,128]{2,0,1:T(8,128)S(1)} %bitcast.5) | data formatting | bytes 196608
Async XLA Ops:
  0.6 0.9 %copy-start = (f32[32,6,128]{2,0,1:T(8,128)S(1)}, f32[32,6,128]{2,0,1:T(8,128)}, u32[]{:S(2)}) copy-start(f32[32,6,128]{2,0,1:T(8,128)} %param.5) | copy-start | bytes 294916
  1.5 0.7 %copy-start.1 = (s32[32,4]{0,1:T(4,128)S(1)}, s32[32,4]{0,1:T(4,128)}, u32[]{:S(2)}) copy-start(s32[32,4]{0,1:T(4,128)} %param.4) | copy-start | bytes 1540
